TPU v7x, 768 devices: a whole 4x8x12 slice. The times are simulated.
768 devices in a mesh: shard: 32 (over x, y), rep: 24 (over z, core).
Axes of the slice: x: 4, y: 8, z: 12, core: 2. Of those that a mesh axis runs over, the one named last changes fastest.
Arguments:
- acts: bfloat16 [24, 384, 96, 512], P('rep', 'shard'), may hold values from -70 to 70, as said below
- cotangents: bfloat16 [24, 384, 96, 512], P('rep', 'shard'), may hold values from -6 to 6
- block_shapes: int32 [384, 2], P('shard'), may hold values from 128 to 512, as said below
- owners: int32 [768], P('shard'), may hold values from 0 to 23, as said below
Outputs:
- updates: float32 [32, 24, 256, 512], P(None, 'rep', 'shard')
Inputs may be any that keep to these rules, and one draw needn't show every extreme that they name: `acts`: each layer input is within the range; feature columns have different scales. `block_shapes`: live rows and columns of a block; some blocks are full in every draw. Within each group of 24 consecutive factors (factor k of the group, k from 0), owners equals (k + c) mod 24 for one number c of that group.
All inputs are finite; a program needn't handle non-finite values.
Results may differ from a plain program's by a relative error of at most 0.015.
Values may be sent and summed in bfloat16 or wider, within the bound.
A program may use at most 32 MiB of HBM per device.

v0:
```python
import math

import jax
import jax.numpy as jnp
from jax import lax
from jax.sharding import PartitionSpec as P

ITERS = 2


damping_ratio = 0.01


def shifted(array, axis, by):
    count = lax.axis_size(axis)
    return lax.ppermute(array, axis, [(i, (i + by) % count) for i in range(count)])


def inverse_root(stat, block_width):
    identity = jnp.eye(block_width, dtype=jnp.float32)
    damped = stat + damping_ratio * (jnp.trace(stat) / block_width + 1e-06) * identity
    scale_norm = jnp.sqrt(jnp.sum(damped * damped))
    coupled = damped / scale_norm
    estimate = identity * scale_norm ** (-0.25)
    for iteration in range(ITERS):
        factor = (5.0 * identity - coupled) / 4.0
        estimate = jnp.dot(estimate, factor, precision=lax.Precision.HIGHEST)
        square = jnp.dot(factor, factor, precision=lax.Precision.HIGHEST)
        fourth = jnp.dot(square, square, precision=lax.Precision.HIGHEST)
        coupled = jnp.dot(fourth, coupled, precision=lax.Precision.HIGHEST)
    return estimate.astype(jnp.bfloat16)


def token_gradient(inputs, outputs):
    return jnp.einsum("tb,tc->bc", inputs, outputs, preferred_element_type=jnp.float32)


def local(acts, cotangents, block_shapes, owners):
    n_rep = lax.axis_size("rep")
    rep_index = lax.axis_index("rep")
    block_width = acts.shape[3]
    half_rows = block_width // 2
    tokens = acts.shape[2]
    half_tokens = tokens // 2
    offset = owners[0]
    slot_ids = jnp.arange(n_rep, dtype=jnp.int32)
    slot_factor = (slot_ids - offset) % n_rep
    slot_block = slot_factor // 2
    own_factor = (rep_index - offset) % n_rep
    factor_side = own_factor % 2
    own_block = own_factor // 2
    limits = block_shapes[own_block]
    column = jnp.arange(block_width, dtype=jnp.int32)
    keep_inputs = column < limits[0]
    keep_outputs = column < limits[1]
    sent_acts = jnp.take(acts[0], slot_block, axis=0)
    sent_cots = jnp.take(cotangents[0], slot_block, axis=0)
    got_acts, got_cots = (
        lax.all_to_all(sent_acts, "rep", split_axis=0, concat_axis=1, tiled=True),
        lax.all_to_all(sent_cots, "rep", split_axis=0, concat_axis=1, tiled=True),
    )
    inputs = jnp.where(keep_inputs, got_acts[0], 0).reshape(n_rep, tokens, block_width)
    outputs = jnp.where(keep_outputs, got_cots[0], 0).reshape(n_rep, tokens, block_width)
    first_part = token_gradient(
        inputs[:, :half_tokens].reshape(-1, block_width),
        outputs[:, :half_tokens].reshape(-1, block_width),
    ).astype(jnp.bfloat16)
    second_part = token_gradient(
        inputs[:, half_tokens:].reshape(-1, block_width),
        outputs[:, half_tokens:].reshape(-1, block_width),
    ).astype(jnp.bfloat16)
    gradient = first_part.astype(jnp.float32) + second_part.astype(jnp.float32)
    grad_bf = gradient.astype(jnp.bfloat16)
    left_factor = jnp.where(factor_side == 0, grad_bf, grad_bf.T)
    stat = jnp.dot(left_factor, left_factor.T, preferred_element_type=jnp.float32)
    root_bf = inverse_root(stat, block_width)
    next_full = shifted(root_bf, "rep", -1)
    prev_lower = shifted(root_bf[half_rows:], "rep", 1)
    left_rows = jnp.where(factor_side == 0, root_bf[:half_rows], prev_lower)
    right_root = jnp.where(factor_side == 0, next_full, root_bf)
    product = jnp.dot(left_rows, grad_bf, preferred_element_type=jnp.float32).astype(jnp.bfloat16)
    update_rows = math.sqrt(block_width) * jnp.dot(
        product, right_root, preferred_element_type=jnp.float32
    )
    return lax.all_to_all(update_rows[None, None], "shard", split_axis=2, concat_axis=0, tiled=True)


def solution(mesh):
    return jax.shard_map(
        local,
        mesh=mesh,
        in_specs=(
            P("rep", "shard", None, None),
            P("rep", "shard", None, None),
            P("shard", None),
            P("shard"),
        ),
        out_specs=P(None, "rep", "shard", None),
        check_vma=False,
    )
```

profile of v0, /device:TPU:8, one launch (start us, length us, event | category | flops | bytes accessed | tf_op | source)
XLA Modules:
  0.0 248.5 jit_solution(13893600507420551596)
XLA Ops:
  0.0 0.0 copy-start
  0.0 0.8 compare_and_fusion
  0.8 0.7 compare_select_fusion
  1.5 0.0 copy-done
  1.5 0.7 gather_fusion.1
  2.2 3.5 %gather_fusion = bf16[24,96,512]{2,1,0:T(8,128)(2,1)} fusion(bf16[12,96,512]{2,1,0:T(8,128)(2,1)} %bitcast.37, s32[1024]{0:T(1024)S(1)} %pad_clamp_fusion), kind=kCustom, calls=%fused_computation.clone | custom fusion | bytes 4718688 | tf_op jit(solution)/shard_map/jit(_take)/gather | solution.py:56
  5.6 3.6 %broadcast_select_fusion.1 = (bf16[24,96,512]{2,1,0:T(8,128)(2,1)S(1)}, bf16[24,96,512]{2,1,0:T(8,128)(2,1)}) fusion(bf16[24,96,512]{2,1,0:T(8,128)(2,1)} %gather_fusion, pred[24]{0:T(512)(128)(4,1)S(1)} %compare_and_fusion, bf16[24,96,512]{2,1,0:T(8,128)(2,1)S(1)} %gather_fusion.1), kind=kLoop, calls=%fused_computation.3 | loop fusion | flops 2359296 | bytes 9437208 | tf_op jit(solution)/shard_map/jit(_take)/select_n | solution.py:56
  9.2 98.9 %all_to_all.30 = bf16[24,96,512]{2,1,0:T(8,128)(2,1)} all-to-all(bf16[24,96,512]{2,1,0:T(8,128)(2,1)S(1)} %get-tuple-element.8), channel_id=1, replica_groups=mesh['shard'=32,'rep'=24] {'rep'}, dimensions={0} | all-to-all | bytes 4718592 | tf_op jit(solution)/shard_map/all_to_all | solution.py:59
  108.1 0.0 copy-start.5
  108.1 0.0 copy-start.4
  108.1 4.2 %all-to-all-start.1 = ((bf16[24,96,512]{2,1,0:T(8,128)(2,1)}), bf16[24,96,512]{2,1,0:T(8,128)(2,1)S(1)}, u32[]{:S(2)}, u32[]{:S(2)}) async-start(bf16[24,96,512]{2,1,0:T(8,128)(2,1)} %get-tuple-element.9), calls=%async_computation.1 | async-start | bytes 4718592 | tf_op jit(solution)/shard_map/all_to_all | solution.py:60
  112.2 0.0 copy-done.5
  112.3 0.0 copy-done.4
  112.3 0.1 constant_dynamic-slice_fusion
  112.4 0.6 fusion.41
  113.0 0.6 iota_compare_fusion.3
  113.7 0.7 iota_compare_fusion.2
  114.4 3.2 %broadcast_select_fusion.3 = bf16[24,96,512]{2,1,0:T(8,128)(2,1)} fusion(bf16[24,96,512]{2,1,0:T(8,128)(2,1)} %all_to_all.30, pred[512]{0:T(512)(128)(4,1)S(1)} %iota_compare_fusion.3), kind=kLoop, calls=%fused_computation.5 | loop fusion | flops 1179648 | bytes 4719104 | tf_op jit(solution)/shard_map/jit(_where)/select_n | solution.py:62
  117.6 77.7 %all-to-all-done.1 = bf16[24,96,512]{2,1,0:T(8,128)(2,1)S(1)} async-done(((bf16[24,96,512]{2,1,0:T(8,128)(2,1)}), bf16[24,96,512]{2,1,0:T(8,128)(2,1)S(1)}, u32[]{:S(2)}, u32[]{:S(2)}) %all-to-all-start.1) | async-done | bytes 2359328 | tf_op jit(solution)/shard_map/all_to_all | solution.py:60
  195.3 0.0 copy-start.1
  195.3 0.2 broadcast_select_fusion.2
  195.4 1.5 copy-done.1
  196.9 0.9 fusion.6
  197.8 0.9 fusion.4
  198.7 0.0 copy-start.2
  198.7 0.2 copy.7
  198.9 1.1 select_reduce_fusion
  200.5 0.9 multiply_reduce_fusion
  201.4 0.0 copy-done.2
  202.0 2.0 fusion.16
  204.1 1.9 fusion.13
  206.0 1.8 fusion.42
  207.8 1.9 fusion
  209.7 0.0 copy-start.3
  209.8 1.8 convolution_convert_fusion
  211.6 0.0 collective-permute-start.1
  211.7 0.5 collective-permute-start
  212.2 6.5 %collective-permute-done = bf16[256,512]{1,0:T(8,128)(2,1)S(1)} collective-permute-done((bf16[256,512]{1,0:T(8,128)(2,1)S(1)}, bf16[256,512]{1,0:T(8,128)(2,1)S(1)}, u32[]{:S(2)}, u32[]{:S(2)}) %collective-permute-start) | collective-permute-done | bytes 262176 | tf_op jit(solution)/shard_map/ppermute | solution.py:16
  218.7 0.0 collective-permute-done.1
  218.7 0.0 copy-done.3
  218.7 0.5 fusion.7
  219.2 0.5 copy.8
  219.8 27.9 %all_to_all.31 = f32[1,1,256,512]{3,1,0,2:T(1,128)S(1)} all-to-all(f32[1,1,256,512]{3,1,0,2:T(1,128)S(1)} %copy.8), channel_id=1, replica_groups=mesh['shard'=32,'rep'=24] {'shard'}, dimensions={2} | all-to-all | bytes 1048576 | tf_op jit(solution)/shard_map/all_to_all | solution.py:85
  247.6 0.8 copy.9
  (2 shorter events, 0.0 us)
Async XLA Ops:
  0.0 1.5 copy-start
  108.1 4.2 %copy-start.5 = (s32[24]{0:T(128)S(1)}, s32[24]{0:T(128)}, u32[]{:S(2)}) copy-start(s32[24]{0:T(128)} %param.9) | copy-start | bytes 292
  108.1 4.3 %copy-start.4 = (s32[12,2]{0,1:T(2,128)S(1)}, s32[12,2]{0,1:T(2,128)}, u32[]{:S(2)}) copy-start(s32[12,2]{0,1:T(2,128)} %param.8) | copy-start | bytes 292
  108.1 87.2 %all-to-all-start.1 = ((bf16[24,96,512]{2,1,0:T(8,128)(2,1)}), bf16[24,96,512]{2,1,0:T(8,128)(2,1)S(1)}, u32[]{:S(2)}, u32[]{:S(2)}) async-start(bf16[24,96,512]{2,1,0:T(8,128)(2,1)} %get-tuple-element.9), calls=%async_computation.1 | async-start | bytes 4718592 | tf_op jit(solution)/shard_map/all_to_all | solution.py:60
  195.3 1.7 copy-start.1
  198.7 2.7 %copy-start.2 = (bf16[512,512]{1,0:T(8,128)(2,1)}, bf16[512,512]{1,0:T(8,128)(2,1)S(1)}, u32[]{:S(2)}) copy-start(bf16[512,512]{1,0:T(8,128)(2,1)S(1)} %fusion.4) | copy-start | bytes 1572868
  209.7 9.0 %copy-start.3 = (bf16[512,512]{1,0:T(8,128)(2,1)S(1)}, bf16[512,512]{1,0:T(8,128)(2,1)}, u32[]{:S(2)}) copy-start(bf16[512,512]{1,0:T(8,128)(2,1)} %copy-done.2) | copy-start | bytes 1572868
  211.6 7.1 %collective-permute-start.1 = (bf16[512,512]{1,0:T(8,128)(2,1)S(1)}, bf16[512,512]{1,0:T(8,128)(2,1)S(1)}, u32[]{:S(2)}, u32[]{:S(2)}) collective-permute-start(bf16[512,512]{1,0:T(8,128)(2,1)S(1)} %convolution_convert_fusion), channel_id=1, source_target_pairs={{0,23},{1,0},{2,1},{3,2},{4,3},{5,4},{6,5},{7,6},{8,7},{9,8},{10,9... | collective-permute-start | bytes 1572872 | tf_op jit(solution)/shard_map/ppermute | solution.py:16
  211.7 7.0 %collective-permute-start = (bf16[256,512]{1,0:T(8,128)(2,1)S(1)}, bf16[256,512]{1,0:T(8,128)(2,1)S(1)}, u32[]{:S(2)}, u32[]{:S(2)}) collective-permute-start(bf16[256,512]{1,0:T(8,128)(2,1)S(1)} %slice.47), channel_id=1, source_target_pairs={{0,1},{1,2},{2,3},{3,4},{4,5},{5,6},{6,7},{7,8},{8,9},{9,10},{10,1... | collective-permute-start | bytes 786440 | tf_op jit(solution)/shard_map/ppermute | solution.py:16
where the time goes:
time: 249 us; the launch traced here: 248 us
  blocking collectives  127 us (51%)
  waiting for transfers between devices  84.2 us (34%)
  matrix products  12.8 us (5%)
  other arithmetic  10.6 us (4%)
  local copies, waits for them, and re-layouts  7.94 us (3%)
  starting transfers between devices  4.69 us (2%)
    all_to_all x1, blocking collectives, local(): lax.all_to_all(sent_acts, 'rep', split_axis=0, concat_axis=1, tiled=True)  98.9 us
    all_to_all x1, waiting for transfers between devices, local(): lax.all_to_all(sent_cots, 'rep', split_axis=0, concat_axis=1, tiled=True)  77.7 us
    all_to_all x1, blocking collectives, local(): lax.all_to_all(update_rows[None, None], 'shard', split_axis=2, concat_axi...  27.9 us
    ppermute x2, waiting for transfers between devices, shifted(): lax.ppermute(array, axis, [(i, (i + by) % count) for i in range(count)])  6.52 us
  transfers between devices with their start and end apart: 3, of which 2 were waited for; matrix products, arithmetic and copies ran while one was open for 2% of the time, Pallas kernels for 0%

commit v1 on v0

v1 whole, which is shorter than its diff:
```python
import functools
import math

import jax
import jax.numpy as jnp
from jax import lax
from jax.experimental import pallas as pl
from jax.experimental.pallas import tpu as pltpu
from jax.sharding import PartitionSpec as P

MESH = pl.DeviceIdType.MESH
DAMPING = 0.01
CHUNKS = 4
STRIPS = 4

ROWS_BY_ROWS = (((1,), (1,)), ((), ()))
COLUMNS_BY_COLUMNS = (((0,), (0,)), ((), ()))


def dot(a, b, dims=(((1,), (0,)), ((), ()))):
    return lax.dot_general(a, b, dims, preferred_element_type=jnp.float32)


def kernel(
    n_z, n_x, n_y,
    owners_ref, shapes_ref, acts_ref, cots_ref, out_ref,
    staged, paired, part_long, part_short, in_long, in_short, grad,
    stat, coupled, coupled_bf, work, work_bf, left, right,
    weighted, weighted_out, rows_own, rows_shift, rows_out, landing,
    pair_send, pair_recv, long_send, long_recv, short_send, short_recv,
    grad_send, grad_recv, root_send, root_recv, shift_send, shift_recv, rows_send, rows_recv,
):
    width = acts_ref.shape[3]
    tokens = acts_ref.shape[2]
    half = width // 2
    n_shard = n_x * n_y
    n_long = n_z // 2
    n_short = n_z - 1 - n_long
    shard = lax.axis_index("shard")
    rep = lax.axis_index("rep")
    z = rep // 2
    core = rep % 2
    x = shard // n_y
    y = shard % n_y
    sign = 1 - 2 * core
    partner = (shard, z * 2 + 1 - core)
    long_to = (shard, lax.rem(z + sign + n_z, n_z) * 2 + core)
    short_to = (shard, lax.rem(z - sign + n_z, n_z) * 2 + core)
    shift_to = (shard, lax.rem(z + 1, n_z) * 2 + core)
    shift_from = (shard, lax.rem(z + n_z - 1, n_z) * 2 + core)

    def peer(across, along):
        return lax.rem(x + across, n_x) * n_y + lax.rem(y + along, n_y)

    def source(across, along):
        return lax.rem(x + n_x - across, n_x) * n_y + lax.rem(y + n_y - along, n_y)

    barrier = pltpu.get_barrier_semaphore()
    for neighbour in (partner, long_to, short_to):
        pl.semaphore_signal(barrier, inc=1, device_id=neighbour, device_id_type=MESH)

    @pl.loop(1, n_shard)
    def _(step):
        to = (peer(step // n_y, lax.rem(step, n_y)), rep)
        pl.semaphore_signal(barrier, inc=1, device_id=to, device_id_type=MESH)

    rotation = owners_ref[0]
    turn = lax.div(rotation, 2)
    odd = (rotation - 2 * turn).astype(jnp.float32)
    even = 1.0 - odd

    def block_of(chip):
        return lax.rem(chip + 2 * n_z - turn, n_z)

    def hops(item):
        pair, second = lax.div(item, 2), lax.rem(item, 2)
        return (1 - second) * (n_long - pair) - second * (n_short - pair)

    own_columns = pl.ds(pl.multiple_of(core * half, half), half)
    other_columns = pl.ds(pl.multiple_of((1 - core) * half, half), half)

    @pl.loop(0, n_z)
    def _(item):
        block = block_of(lax.rem(z - sign * hops(item) + n_z, n_z))
        staged[item, :, :width] = cots_ref[0, block]
        staged[item, :, width:] = acts_ref[0, block, :, other_columns]

    def pair_copy(item):
        return pltpu.make_async_remote_copy(
            src_ref=staged.at[item],
            dst_ref=paired.at[item, pl.ds(tokens, tokens), :],
            send_sem=pair_send.at[item],
            recv_sem=pair_recv.at[item],
            device_id=partner,
            device_id_type=MESH,
        )

    pl.semaphore_wait(barrier, 3 + n_shard - 1)

    @pl.loop(0, n_z)
    def _(item):
        pair_copy(item).start()

    @pl.loop(0, n_z)
    def _(item):
        block = block_of(lax.rem(z + sign * hops(item) + n_z, n_z))
        paired[item, :tokens, :width] = cots_ref[0, block]
        paired[item, :tokens, width:] = acts_ref[0, block, :, own_columns]

    def partial(item, into):
        pair_copy(item).wait_recv()
        into[...] = dot(paired[item, :, width:], paired[item, :, :width], COLUMNS_BY_COLUMNS)

    rows = half // CHUNKS

    def ring_copy(buffer, send, recv, to, step, chunk):
        return pltpu.make_async_remote_copy(
            src_ref=buffer.at[step, pl.ds(chunk * rows, rows), :],
            dst_ref=buffer.at[step + 1, pl.ds(chunk * rows, rows), :],
            send_sem=send.at[step, chunk],
            recv_sem=recv.at[step, chunk],
            device_id=to,
            device_id_type=MESH,
        )

    long_copy = functools.partial(ring_copy, in_long, long_send, long_recv, long_to)
    short_copy = functools.partial(ring_copy, in_short, short_send, short_recv, short_to)

    partial(0, part_long)
    for chunk in range(CHUNKS):
        span = pl.ds(chunk * rows, rows)
        in_long[0, span, :] = part_long[span, :].astype(jnp.bfloat16)
        long_copy(0, chunk).start()
    partial(1, part_short)
    for chunk in range(CHUNKS):
        span = pl.ds(chunk * rows, rows)
        in_short[0, span, :] = part_short[span, :].astype(jnp.bfloat16)
        short_copy(0, chunk).start()

    def forward(buffer, part, copy, step, chunk):
        span = pl.ds(chunk * rows, rows)
        copy(step - 1, chunk).wait_recv()
        total = buffer[step, span, :].astype(jnp.float32) + part[span, :]
        buffer[step, span, :] = total.astype(jnp.bfloat16)
        copy(step, chunk).start()

    @pl.loop(1, n_short)
    def _(step):
        partial(2 * step, part_long)
        partial(2 * step + 1, part_short)
        for chunk in range(CHUNKS):
            forward(in_long, part_long, long_copy, step, chunk)
            forward(in_short, part_short, short_copy, step, chunk)

    partial(2 * n_long - 2, part_long)
    partial(2 * n_long - 1, part_short)
    for chunk in range(CHUNKS):
        forward(in_long, part_long, long_copy, n_long - 1, chunk)

    own_block = block_of(z)
    live_rows = shapes_ref[own_block, 0]
    live_columns = shapes_ref[own_block, 1]

    def grad_copy(chunk):
        span = pl.ds(pl.multiple_of(core * half + chunk * rows, rows), rows)
        return pltpu.make_async_remote_copy(
            src_ref=grad.at[span, :],
            dst_ref=grad.at[span, :],
            send_sem=grad_send.at[chunk],
            recv_sem=grad_recv.at[chunk],
            device_id=partner,
            device_id_type=MESH,
        )

    for chunk in range(CHUNKS):
        span = pl.ds(chunk * rows, rows)
        short_copy(n_short - 1, chunk).wait_recv()
        total = part_short[span, :] + in_short[n_short, span, :].astype(jnp.float32)
        long_copy(n_long - 1, chunk).wait_recv()
        total = total + in_long[n_long, span, :].astype(jnp.float32)
        first = core * half + chunk * rows
        below = live_rows - first - lax.broadcasted_iota(jnp.int32, (rows, width), 0)
        before = live_columns - lax.broadcasted_iota(jnp.int32, (rows, width), 1)
        live = jnp.minimum(jnp.maximum(jnp.minimum(below, before), 0), 1)
        total = total * live.astype(jnp.float32)
        grad[pl.ds(pl.multiple_of(first, rows), rows), :] = total.astype(jnp.bfloat16)
        grad_copy(chunk).start()
    for chunk in range(CHUNKS):
        grad_copy(chunk).wait_recv()

    deep = width // STRIPS
    strips = [slice(i * deep, (i + 1) * deep) for i in range(STRIPS)]

    @pl.when(core == 0)
    def _():
        for strip in strips:
            stat[strip, :] = dot(grad[strip, :], grad[...], ROWS_BY_ROWS)

    @pl.when(core == 1)
    def _():
        for strip in strips:
            stat[strip, :] = dot(grad[:, strip], grad[...], COLUMNS_BY_COLUMNS)

    def diagonal(strip):
        return (
            lax.broadcasted_iota(jnp.int32, (deep, width), 0) + strip.start
            == lax.broadcasted_iota(jnp.int32, (deep, width), 1)
        )

    squares = jnp.zeros((1, 1), jnp.float32)
    trace = jnp.zeros((1, 1), jnp.float32)
    for strip in strips:
        values = stat[strip, :]
        squares += jnp.sum(values * values, keepdims=True)
        trace += jnp.sum(jnp.where(diagonal(strip), values, 0.0), keepdims=True)
    damping = DAMPING * (trace / width + 1e-06)
    norm_squared = squares + damping * (2.0 * trace + width * damping)
    inverse = lax.rsqrt(norm_squared)
    scale = lax.rsqrt(jnp.sqrt(jnp.sqrt(norm_squared)))

    for strip in strips:
        values = (stat[strip, :] + jnp.where(diagonal(strip), damping, 0.0)) * inverse
        coupled[strip, :] = values
        coupled_bf[strip, :] = values.astype(jnp.bfloat16)
    for strip in strips:
        square = dot(coupled_bf[strip, :], coupled_bf[...])
        values = 0.0625 * square - 0.625 * coupled[strip, :]
        stat[strip, :] = values
        work_bf[0, strip, :] = values.astype(jnp.bfloat16)
    for strip in strips:
        square = dot(work_bf[0, strip, :], work_bf[0])
        work_bf[1, strip, :] = (square + 3.125 * stat[strip, :]).astype(jnp.bfloat16)
    for strip in strips:
        values = dot(work_bf[1, strip, :], coupled_bf[...]) + 2.44140625 * coupled[strip, :]
        work[strip, :] = values
        work_bf[0, strip, :] = values.astype(jnp.bfloat16)

    def root(strip):
        values = 0.0625 * dot(coupled_bf[strip, :], work_bf[0])
        values = values - 0.3125 * (coupled[strip, :] + work[strip, :])
        values = values + jnp.where(diagonal(strip), 1.5625, 0.0)
        return (values * scale).astype(jnp.bfloat16)

    def right_copy(index):
        span = pl.ds(index * deep, deep)
        return pltpu.make_async_remote_copy(
            src_ref=right.at[span, :],
            dst_ref=right.at[span, :],
            send_sem=root_send.at[index],
            recv_sem=root_recv.at[index],
            device_id=partner,
            device_id_type=MESH,
        )

    weighted_copy = pltpu.make_async_remote_copy(
        src_ref=weighted_out,
        dst_ref=weighted,
        send_sem=root_send.at[STRIPS],
        recv_sem=root_recv.at[STRIPS],
        device_id=partner,
        device_id_type=MESH,
    )

    @pl.when(core == 1)
    def _():
        for index, strip in enumerate(strips):
            right[strip, :] = root(strip)
            right_copy(index).start()
        weighted_copy.wait_recv()

    @pl.when(core == 0)
    def _():
        for strip in strips:
            left[strip, :] = root(strip)
        upper = left[:half, :].astype(jnp.float32)
        lower = left[half:, :].astype(jnp.float32)
        given = (upper * odd + lower * even).astype(jnp.bfloat16)
        weighted_out[...] = dot(given, grad[...]).astype(jnp.bfloat16)
        weighted_copy.start()
        kept = (upper * even + lower * odd).astype(jnp.bfloat16)
        weighted[...] = dot(kept, grad[...]).astype(jnp.bfloat16)
        for index in range(STRIPS):
            right_copy(index).wait_recv()

    piece = half // n_shard
    spread = half // n_x

    def update_rows(across):
        start = pl.multiple_of(lax.rem(x + across, n_x) * spread, spread)
        values = dot(weighted[pl.ds(start, spread), :], right[...]) * math.sqrt(width)
        values = values.reshape(n_y, piece, width)
        values = jnp.concatenate([values[:, :, :half], values[:, :, half:]], axis=1)
        return values.astype(jnp.bfloat16)

    def places(across):
        start = pl.multiple_of(lax.rem(x + across, n_x) * n_y, n_y)
        return pl.ds(start, n_y)

    def shift_copy(across):
        return pltpu.make_async_remote_copy(
            src_ref=rows_own.at[places(across)],
            dst_ref=rows_shift.at[places(across)],
            send_sem=shift_send.at[across],
            recv_sem=shift_recv.at[across],
            device_id=shift_to,
            device_id_type=MESH,
        )

    def rows_copy(across, along):
        return pltpu.make_async_remote_copy(
            src_ref=rows_out.at[peer(across, along)],
            dst_ref=landing.at[shard],
            send_sem=rows_send.at[across, along],
            recv_sem=rows_recv.at[across, along],
            device_id=(peer(across, along), rep),
            device_id_type=MESH,
        )

    def spread_rows(across):
        if across == 0:
            landing[shard] = rows_out[shard]

        @pl.loop(1 if across == 0 else 0, n_y)
        def _(along):
            rows_copy(across, along).start()

    @pl.when(core == 1)
    def _():
        for across in range(n_x):
            rows_out[places(across)] = update_rows(across)
            spread_rows(across)

    @pl.when(core == 0)
    def _():
        for across in range(n_x):
            rows_own[places(across)] = update_rows(across)
            shift_copy(across).start()
        for across in range(n_x):
            shift_copy(across).wait_recv()
            moved = rows_shift[places(across)].astype(jnp.float32)
            values = moved * odd + rows_own[places(across)].astype(jnp.float32) * even
            rows_out[places(across)] = values.astype(jnp.bfloat16)
            spread_rows(across)

    def unfold(place):
        values = landing[place].astype(jnp.float32)
        out_ref[place, 0, :, :half] = values[:piece]
        out_ref[place, 0, :, half:] = values[piece:]

    unfold(shard)

    @pl.loop(1, n_shard)
    def _(step):
        across, along = step // n_y, lax.rem(step, n_y)
        rows_copy(across, along).wait_recv()
        unfold(source(across, along))

    @pl.loop(0, n_z)
    def _(item):
        pair_copy(item).wait_send()

    @pl.loop(0, n_long)
    def _(step):
        for chunk in range(CHUNKS):
            long_copy(step, chunk).wait_send()

    @pl.loop(0, n_short)
    def _(step):
        for chunk in range(CHUNKS):
            short_copy(step, chunk).wait_send()

    for chunk in range(CHUNKS):
        grad_copy(chunk).wait_send()

    @pl.when(core == 1)
    def _():
        for index in range(STRIPS):
            right_copy(index).wait_send()

    @pl.when(core == 0)
    def _():
        weighted_copy.wait_send()
        for across in range(n_x):
            shift_copy(across).wait_send()

    @pl.loop(1, n_shard)
    def _(step):
        rows_copy(step // n_y, lax.rem(step, n_y)).wait_send()


def local(n_shard, n_rep, acts, cotangents, block_shapes, owners):
    n_z = n_rep // 2
    n_x = 4 if n_shard == 32 else 1
    n_y = n_shard // n_x
    tokens, width = acts.shape[2:]
    half = width // 2
    n_long = n_z // 2
    n_short = n_z - 1 - n_long
    piece = half // n_shard
    bf16, f32 = jnp.bfloat16, jnp.float32
    dma = pltpu.SemaphoreType.DMA
    pieces = pltpu.VMEM((n_shard, 2 * piece, half), bf16)
    return pl.pallas_call(
        functools.partial(kernel, n_z, n_x, n_y),
        out_shape=jax.ShapeDtypeStruct((n_shard, 1, piece, width), f32),
        in_specs=[pl.BlockSpec(memory_space=pltpu.SMEM)] * 2 + [pl.BlockSpec(memory_space=pltpu.VMEM)] * 2,
        out_specs=pl.BlockSpec(memory_space=pltpu.VMEM),
        scratch_shapes=[
            pltpu.VMEM((n_z, tokens, width + half), bf16),
            pltpu.VMEM((n_z, 2 * tokens, width + half), bf16),
            pltpu.VMEM((half, width), f32),
            pltpu.VMEM((half, width), f32),
            pltpu.VMEM((n_long + 1, half, width), bf16),
            pltpu.VMEM((n_short + 1, half, width), bf16),
            pltpu.VMEM((width, width), bf16),
            pltpu.VMEM((width, width), f32),
            pltpu.VMEM((width, width), f32),
            pltpu.VMEM((width, width), bf16),
            pltpu.VMEM((width, width), f32),
            pltpu.VMEM((2, width, width), bf16),
            pltpu.VMEM((width, width), bf16),
            pltpu.VMEM((width, width), bf16),
            pltpu.VMEM((half, width), bf16),
            pltpu.VMEM((half, width), bf16),
            pieces,
            pieces,
            pieces,
            pieces,
            dma((n_z,)),
            dma((n_z,)),
            dma((n_long, CHUNKS)),
            dma((n_long, CHUNKS)),
            dma((n_short, CHUNKS)),
            dma((n_short, CHUNKS)),
            dma((CHUNKS,)),
            dma((CHUNKS,)),
            dma((STRIPS + 1,)),
            dma((STRIPS + 1,)),
            dma((n_x,)),
            dma((n_x,)),
            dma((n_x, n_y)),
            dma((n_x, n_y)),
        ],
        compiler_params=pltpu.CompilerParams(
            collective_id=0, has_side_effects=True, vmem_limit_bytes=40 * 1024 * 1024
        ),
    )(owners, block_shapes, acts, cotangents)


def solution(mesh):
    return jax.shard_map(
        functools.partial(local, mesh.shape["shard"], mesh.shape["rep"]),
        mesh=mesh,
        in_specs=(
            P("rep", "shard", None, None),
            P("rep", "shard", None, None),
            P("shard", None),
            P("shard"),
        ),
        out_specs=P(None, "rep", "shard", None),
        check_vma=False,
    )
```

time: 249 us -> 76.9 us (0.31)
  the two profiles are of different devices: /device:TPU:8 before, /device:TPU:16 now
where the time goes in v1:
time: 76.9 us; the launch traced here: 76.6 us
  Pallas kernels  71.9 us (93%)
  local copies, waits for them, and re-layouts  4.76 us (6%)
    pallas_call x1, Pallas kernels, local(): pl.pallas_call(functools.partial(kernel, n_z, n_x, n_y), out_shape=jax.Sh...  71.9 us
    unnamed x8, local copies, waits for them, and re-layouts  4.76 us

profile of v1, /device:TPU:16, one launch (start us, length us, event | category | flops | bytes accessed | tf_op | source)
XLA Modules:
  0.0 76.6 jit_solution(7041723712178055056)
XLA Ops:
  0.0 0.8 copy.5.shapes_ref
  0.8 0.0 copy-start
  0.8 1.3 %copy-done = bf16[1,12,96,512]{3,2,1,0:T(8,128)(2,1)S(1)} copy-done((bf16[1,12,96,512]{3,2,1,0:T(8,128)(2,1)S(1)}, bf16[1,12,96,512]{3,2,1,0:T(8,128)(2,1)}, u32[]{:S(2)}) %copy-start) | copy-done | bytes 1179672
  2.0 0.0 copy-start.1
  2.0 1.3 %copy-done.1 = bf16[1,12,96,512]{3,2,1,0:T(8,128)(2,1)S(1)} copy-done((bf16[1,12,96,512]{3,2,1,0:T(8,128)(2,1)S(1)}, bf16[1,12,96,512]{3,2,1,0:T(8,128)(2,1)}, u32[]{:S(2)}) %copy-start.1) | copy-done | bytes 1179672
  3.3 0.0 copy-start.2
  3.3 0.7 copy-done.2
  4.0 71.9 %shard_map.46 = f32[32,1,8,512]{3,2,1,0:T(8,128)S(1)} custom-call(s32[24]{0:T(128)S(1)} %copy-done.2, s32[12,2]{1,0:T(8,128)S(1)} %copy.5.shapes_ref, bf16[1,12,96,512]{3,2,1,0:T(8,128)(2,1)S(1)} %copy-done, bf16[1,12,96,512]{3,2,1,0:T(8,128)(2,1)S(1)} %copy-done.1), custom_call_target="tpu_custom_call" | custom-call | tf_op jit(solution)/shard_map/pallas_call | solution.py:403
  75.9 0.8 %copy.7 = f32[32,1,8,512]{3,2,1,0:T(8,128)} copy(f32[32,1,8,512]{3,2,1,0:T(8,128)S(1)} %shard_map.46) | data formatting | bytes 1048576
Async XLA Ops:
  0.8 1.3 %copy-start = (bf16[1,12,96,512]{3,2,1,0:T(8,128)(2,1)S(1)}, bf16[1,12,96,512]{3,2,1,0:T(8,128)(2,1)}, u32[]{:S(2)}) copy-start(bf16[1,12,96,512]{3,2,1,0:T(8,128)(2,1)} %acts_ref.1) | copy-start | bytes 3538948
  2.0 1.3 %copy-start.1 = (bf16[1,12,96,512]{3,2,1,0:T(8,128)(2,1)S(1)}, bf16[1,12,96,512]{3,2,1,0:T(8,128)(2,1)}, u32[]{:S(2)}) copy-start(bf16[1,12,96,512]{3,2,1,0:T(8,128)(2,1)} %cots_ref.1) | copy-start | bytes 3538948
  3.3 0.7 copy-start.2

commit v2 on v1

v2 whole, which is shorter than its diff:
```python
import functools
import math

import jax
import jax.numpy as jnp
from jax import lax
from jax.experimental import pallas as pl
from jax.experimental.pallas import tpu as pltpu
from jax.sharding import PartitionSpec as P

MESH = pl.DeviceIdType.MESH
DAMPING = 0.01
CHUNKS = 8
LOADS = 4
STRIPS = 4

ROWS_BY_ROWS = (((1,), (1,)), ((), ()))
COLUMNS_BY_COLUMNS = (((0,), (0,)), ((), ()))


def dot(a, b, dims=(((1,), (0,)), ((), ()))):
    return lax.dot_general(a, b, dims, preferred_element_type=jnp.float32)


def kernel(
    n_z, n_x, n_y,
    owners_hbm, shapes_hbm, acts_hbm, cots_hbm, out_ref,
    owners_ref, shapes_ref, acts_ref, cots_ref, staged, paired, part, ring, swapped, grad,
    stat, coupled, coupled_bf, work, work_bf, left, right,
    weighted, weighted_out, rows_own, rows_shift, rows_out,
    loaded, pair_send, pair_recv, ring_send, ring_recv,
    swap_send, swap_recv, root_send, root_recv, shift_send, shift_recv, rows_send, rows_recv,
):
    tokens, width = acts_ref.shape[1:]
    half = width // 2
    n_shard = n_x * n_y
    n_hops = n_z // 2
    shard = lax.axis_index("shard")
    rep = lax.axis_index("rep")
    z = rep // 2
    core = rep % 2
    x = shard // n_y
    y = shard % n_y
    sign = 1 - 2 * core
    partner = (shard, z * 2 + 1 - core)
    above = (shard, lax.rem(z + 1, n_z) * 2 + core)
    below = (shard, lax.rem(z + n_z - 1, n_z) * 2 + core)
    ring_to = (shard, lax.rem(z + sign + n_z, n_z) * 2 + core)

    def peer(across, along):
        return lax.rem(x + across, n_x) * n_y + lax.rem(y + along, n_y)

    span = n_z // LOADS
    loads = [
        pltpu.make_async_copy(owners_hbm, owners_ref, loaded.at[2 * LOADS]),
        pltpu.make_async_copy(shapes_hbm, shapes_ref, loaded.at[2 * LOADS + 1]),
    ]
    for index in range(LOADS):
        blocks = pl.ds(index * span, span)
        loads.append(pltpu.make_async_copy(cots_hbm.at[0, blocks], cots_ref.at[blocks], loaded.at[index]))
        loads.append(pltpu.make_async_copy(acts_hbm.at[0, blocks], acts_ref.at[blocks], loaded.at[LOADS + index]))
    for load in loads:
        load.start()

    barrier = pltpu.get_barrier_semaphore()
    for neighbour in (partner, above, below):
        pl.semaphore_signal(barrier, inc=1, device_id=neighbour, device_id_type=MESH)

    @pl.loop(1, n_shard)
    def _(step):
        to = (peer(step // n_y, lax.rem(step, n_y)), rep)
        pl.semaphore_signal(barrier, inc=1, device_id=to, device_id_type=MESH)

    for load in loads:
        load.wait()
    rotation = owners_ref[0]
    turn = lax.div(rotation, 2)
    parity = rotation - 2 * turn
    odd = parity.astype(jnp.float32)
    even = 1.0 - odd

    def block_of(chip):
        return lax.rem(chip + 2 * n_z - turn, n_z)

    def block_at(chip):
        return block_of(lax.rem(chip + n_z, n_z))

    own_tokens = pl.ds(pl.multiple_of(core * tokens, tokens), tokens)

    @pl.loop(0, n_hops + 1)
    def _(item):
        block = block_at(z - sign * (n_hops - item))
        staged[item, :, :width] = cots_ref[block]
        staged[item, :, width:] = acts_ref[block]

    def pair_copy(item):
        return pltpu.make_async_remote_copy(
            src_ref=staged.at[item],
            dst_ref=paired.at[item, own_tokens, :],
            send_sem=pair_send.at[item],
            recv_sem=pair_recv.at[item],
            device_id=partner,
            device_id_type=MESH,
        )

    pl.semaphore_wait(barrier, 3 + n_shard - 1)

    @pl.loop(0, n_hops + 1)
    def _(item):
        pair_copy(item).start()

    def partial(item):
        block = block_at(z + sign * (n_hops - item))
        paired[item, own_tokens, :width] = cots_ref[block]
        paired[item, own_tokens, width:] = acts_ref[block]
        pair_copy(item).wait_recv()
        return paired[item, :, :width]

    rows = width // CHUNKS
    few = CHUNKS // 2

    def span_of(chunk):
        return pl.ds(pl.multiple_of(chunk * rows, rows), rows)

    def ring_copy(step, chunk):
        return pltpu.make_async_remote_copy(
            src_ref=ring.at[step, span_of(chunk), :],
            dst_ref=ring.at[step + 1, span_of(chunk), :],
            send_sem=ring_send.at[step, chunk],
            recv_sem=ring_recv.at[step, chunk],
            device_id=ring_to,
            device_id_type=MESH,
        )

    outputs = partial(0)
    columns = pl.ds(pl.multiple_of(width + core * half, half), half)
    part[:half, :] = dot(paired[0, :, columns], outputs, COLUMNS_BY_COLUMNS)
    for chunk in range(few):
        ring[0, span_of(core * few + chunk), :] = part[chunk * rows : (chunk + 1) * rows, :].astype(jnp.bfloat16)
        ring_copy(0, core * few + chunk).start()

    def all_rows(item):
        outputs = partial(item)
        part[...] = dot(paired[item, :, width:], outputs, COLUMNS_BY_COLUMNS)

    def forward(step, chunk):
        span = span_of(chunk)
        ring_copy(step - 1, chunk).wait_recv()
        total = ring[step, span, :].astype(jnp.float32) + part[span, :]
        ring[step, span, :] = total.astype(jnp.bfloat16)
        ring_copy(step, chunk).start()

    all_rows(1)
    for chunk in range(few):
        place = (1 - core) * few + chunk
        ring[1, span_of(place), :] = part[span_of(place), :].astype(jnp.bfloat16)
        ring_copy(1, place).start()
    for chunk in range(few):
        forward(1, core * few + chunk)

    @pl.loop(2, n_hops)
    def _(step):
        all_rows(step)
        for chunk in range(CHUNKS):
            forward(step, chunk)

    all_rows(n_hops)

    own_block = block_of(z)
    live_rows = shapes_ref[0, own_block]
    live_columns = shapes_ref[1, own_block]

    def swap_copy(chunk):
        return pltpu.make_async_remote_copy(
            src_ref=ring.at[n_hops, span_of(chunk), :],
            dst_ref=swapped.at[span_of(chunk), :],
            send_sem=swap_send.at[chunk],
            recv_sem=swap_recv.at[chunk],
            device_id=partner,
            device_id_type=MESH,
        )

    def gather(chunk):
        span = slice(chunk * rows, (chunk + 1) * rows)
        swap_copy(chunk).wait_recv()
        total = ring[n_hops, span, :].astype(jnp.float32) + swapped[span, :].astype(jnp.float32)
        total = total + part[span, :]
        below_limit = live_rows - chunk * rows - lax.broadcasted_iota(jnp.int32, (rows, width), 0)
        before_limit = live_columns - lax.broadcasted_iota(jnp.int32, (rows, width), 1)
        live = jnp.minimum(jnp.maximum(jnp.minimum(below_limit, before_limit), 0), 1)
        grad[span, :] = (total * live.astype(jnp.float32)).astype(jnp.bfloat16)

    for chunk in range(CHUNKS):
        ring_copy(n_hops - 1, chunk).wait_recv()
        swap_copy(chunk).start()
        if chunk > 0:
            gather(chunk - 1)
    gather(CHUNKS - 1)

    deep = width // STRIPS
    strips = [slice(i * deep, (i + 1) * deep) for i in range(STRIPS)]

    @pl.when(core == 0)
    def _():
        for strip in strips:
            stat[strip, :] = dot(grad[strip, :], grad[...], ROWS_BY_ROWS)

    @pl.when(core == 1)
    def _():
        for strip in strips:
            stat[strip, :] = dot(grad[:, strip], grad[...], COLUMNS_BY_COLUMNS)

    def diagonal(strip):
        return (
            lax.broadcasted_iota(jnp.int32, (deep, width), 0) + strip.start
            == lax.broadcasted_iota(jnp.int32, (deep, width), 1)
        )

    squares = jnp.zeros((1, 1), jnp.float32)
    trace = jnp.zeros((1, 1), jnp.float32)
    for strip in strips:
        values = stat[strip, :]
        squares += jnp.sum(values * values, keepdims=True)
        trace += jnp.sum(jnp.where(diagonal(strip), values, 0.0), keepdims=True)
    damping = DAMPING * (trace / width + 1e-06)
    norm_squared = squares + damping * (2.0 * trace + width * damping)
    inverse = lax.rsqrt(norm_squared)
    scale = lax.rsqrt(jnp.sqrt(jnp.sqrt(norm_squared)))

    for strip in strips:
        values = (stat[strip, :] + jnp.where(diagonal(strip), damping, 0.0)) * inverse
        coupled[strip, :] = values
        coupled_bf[strip, :] = values.astype(jnp.bfloat16)
    for strip in strips:
        square = dot(coupled_bf[strip, :], coupled_bf[...])
        values = 0.0625 * square - 0.625 * coupled[strip, :]
        stat[strip, :] = values
        work_bf[0, strip, :] = values.astype(jnp.bfloat16)
    for strip in strips:
        square = dot(work_bf[0, strip, :], work_bf[0])
        work_bf[1, strip, :] = (square + 3.125 * stat[strip, :]).astype(jnp.bfloat16)
    for strip in strips:
        values = dot(work_bf[1, strip, :], coupled_bf[...]) + 2.44140625 * coupled[strip, :]
        work[strip, :] = values
        work_bf[0, strip, :] = values.astype(jnp.bfloat16)

    def root(strip):
        values = 0.0625 * dot(coupled_bf[strip, :], work_bf[0])
        values = values - 0.3125 * (coupled[strip, :] + work[strip, :])
        values = values + jnp.where(diagonal(strip), 1.5625, 0.0)
        return (values * scale).astype(jnp.bfloat16)

    def right_copy(index):
        span = pl.ds(index * deep, deep)
        return pltpu.make_async_remote_copy(
            src_ref=right.at[span, :],
            dst_ref=right.at[span, :],
            send_sem=root_send.at[index],
            recv_sem=root_recv.at[index],
            device_id=partner,
            device_id_type=MESH,
        )

    weighted_copy = pltpu.make_async_remote_copy(
        src_ref=weighted_out,
        dst_ref=weighted,
        send_sem=root_send.at[STRIPS],
        recv_sem=root_recv.at[STRIPS],
        device_id=partner,
        device_id_type=MESH,
    )

    @pl.when(core == 1)
    def _():
        for index, strip in enumerate(strips):
            right[strip, :] = root(strip)
            right_copy(index).start()
        weighted_copy.wait_recv()

    @pl.when(core == 0)
    def _():
        for index, strip in enumerate(strips):
            place = index % (STRIPS // 2) * deep
            left[index // (STRIPS // 2), place : place + deep, :] = root(strip)
        weighted_out[...] = dot(left[1 - parity], grad[...]).astype(jnp.bfloat16)
        weighted_copy.start()
        weighted[...] = dot(left[parity], grad[...]).astype(jnp.bfloat16)
        for index in range(STRIPS):
            right_copy(index).wait_recv()

    piece = half // n_shard
    spread = half // n_x

    def update_rows(into):
        for across in range(n_x):
            values = dot(weighted[across * spread : (across + 1) * spread, :], right[...]) * math.sqrt(width)
            values = values.reshape(n_y, piece, width)
            values = jnp.concatenate([values[:, :, :half], values[:, :, half:]], axis=1)
            into[:, across] = values.astype(jnp.bfloat16)

    far_first = sorted(range(n_y), key=lambda along: -min(along, n_y - along))
    far_first_x = sorted(range(n_x), key=lambda across: -min(across, n_x - across))

    def column(along):
        return lax.rem(y + along, n_y)

    def shift_copy(along):
        return pltpu.make_async_remote_copy(
            src_ref=rows_own.at[column(along)],
            dst_ref=rows_shift.at[column(along)],
            send_sem=shift_send.at[along],
            recv_sem=shift_recv.at[along],
            device_id=above,
            device_id_type=MESH,
        )

    def rows_copy(across, along):
        return pltpu.make_async_remote_copy(
            src_ref=rows_out.at[column(along), lax.rem(x + across, n_x)],
            dst_ref=out_ref.at[shard],
            send_sem=rows_send.at[across, along],
            recv_sem=rows_recv.at[across, along],
            device_id=(peer(across, along), rep),
            device_id_type=MESH,
        )

    own_copy = pltpu.make_async_copy(rows_out.at[y, x], out_ref.at[shard], rows_send.at[0, 0])

    def send_rows(along):
        for across in far_first_x:
            if (across, along) == (0, 0):
                own_copy.start()
            else:
                rows_copy(across, along).start()

    @pl.when(core == 1)
    def _():
        update_rows(rows_out)
        for along in far_first:
            send_rows(along)

    @pl.when(core == 0)
    def _():
        update_rows(rows_own)
        for along in far_first:
            shift_copy(along).start()
        for along in far_first:
            shift_copy(along).wait_recv()
            place = column(along)
            moved = rows_shift[place].astype(jnp.float32)
            values = moved * odd + rows_own[place].astype(jnp.float32) * even
            rows_out[place] = values.astype(jnp.bfloat16)
            send_rows(along)

    own_copy.wait()

    @pl.loop(1, n_shard)
    def _(step):
        rows_copy(step // n_y, lax.rem(step, n_y)).wait_recv()

    @pl.loop(0, n_hops + 1)
    def _(item):
        pair_copy(item).wait_send()

    for chunk in range(few):
        ring_copy(0, core * few + chunk).wait_send()

    @pl.loop(1, n_hops)
    def _(step):
        for chunk in range(CHUNKS):
            ring_copy(step, chunk).wait_send()

    for chunk in range(CHUNKS):
        swap_copy(chunk).wait_send()

    @pl.when(core == 1)
    def _():
        for index in range(STRIPS):
            right_copy(index).wait_send()

    @pl.when(core == 0)
    def _():
        weighted_copy.wait_send()
        for along in range(n_y):
            shift_copy(along).wait_send()

    for across in range(n_x):
        for along in range(n_y):
            if (across, along) != (0, 0):
                rows_copy(across, along).wait_send()


def local(n_shard, n_rep, acts, cotangents, block_shapes, owners):
    n_z = n_rep // 2
    n_x = 4 if n_shard == 32 else 1
    n_y = n_shard // n_x
    tokens, width = acts.shape[2:]
    half = width // 2
    n_hops = n_z // 2
    piece = half // n_shard
    bf16, f32 = jnp.bfloat16, jnp.float32
    dma = pltpu.SemaphoreType.DMA
    pieces = pltpu.VMEM((n_y, n_x, 2 * piece, half), bf16)
    rows = pl.pallas_call(
        functools.partial(kernel, n_z, n_x, n_y),
        out_shape=pltpu.VMEM((n_shard, 2 * piece, half), bf16),
        in_specs=[pl.BlockSpec(memory_space=pltpu.HBM)] * 4,
        out_specs=pl.BlockSpec(memory_space=pltpu.VMEM),
        scratch_shapes=[
            pltpu.SMEM(owners.shape, jnp.int32),
            pltpu.SMEM(block_shapes.shape[::-1], jnp.int32),
            pltpu.VMEM(acts.shape[1:], bf16),
            pltpu.VMEM(cotangents.shape[1:], bf16),
            pltpu.VMEM((n_hops + 1, tokens, 2 * width), bf16),
            pltpu.VMEM((n_hops + 1, 2 * tokens, 2 * width), bf16),
            pltpu.VMEM((width, width), f32),
            pltpu.VMEM((n_hops + 1, width, width), bf16),
            pltpu.VMEM((width, width), bf16),
            pltpu.VMEM((width, width), bf16),
            pltpu.VMEM((width, width), f32),
            pltpu.VMEM((width, width), f32),
            pltpu.VMEM((width, width), bf16),
            pltpu.VMEM((width, width), f32),
            pltpu.VMEM((2, width, width), bf16),
            pltpu.VMEM((2, half, width), bf16),
            pltpu.VMEM((width, width), bf16),
            pltpu.VMEM((half, width), bf16),
            pltpu.VMEM((half, width), bf16),
            pieces,
            pieces,
            pieces,
            dma((2 * LOADS + 2,)),
            dma((n_hops + 1,)),
            dma((n_hops + 1,)),
            dma((n_hops, CHUNKS)),
            dma((n_hops, CHUNKS)),
            dma((CHUNKS,)),
            dma((CHUNKS,)),
            dma((STRIPS + 1,)),
            dma((STRIPS + 1,)),
            dma((n_y,)),
            dma((n_y,)),
            dma((n_x, n_y)),
            dma((n_x, n_y)),
        ],
        compiler_params=pltpu.CompilerParams(
            collective_id=0, has_side_effects=True, vmem_limit_bytes=62 * 1024 * 1024
        ),
    )(owners, block_shapes.T, acts, cotangents)
    rows = rows.astype(f32).reshape(n_shard, 2, piece, half).transpose(0, 2, 1, 3)
    return rows.reshape(n_shard, 1, piece, width)


def solution(mesh):
    return jax.shard_map(
        functools.partial(local, mesh.shape["shard"], mesh.shape["rep"]),
        mesh=mesh,
        in_specs=(
            P("rep", "shard", None, None),
            P("rep", "shard", None, None),
            P("shard", None),
            P("shard"),
        ),
        out_specs=P(None, "rep", "shard", None),
        check_vma=False,
    )
```

time: 76.9 us -> 72.1 us (0.938)
  the two profiles are of different devices: /device:TPU:16 before, /device:TPU:8 now
where the time goes in v2:
time: 72.1 us; the launch traced here: 71.9 us
  Pallas kernels  71.1 us (99%)
  other arithmetic  0.85 us (1%)
    pallas_call x1, Pallas kernels, local(): pl.pallas_call(functools.partial(kernel, n_z, n_x, n_y), out_shape=pltpu....  71.1 us

profile of v2, /device:TPU:8, one launch (start us, length us, event | category | flops | bytes accessed | tf_op | source)
XLA Modules:
  0.0 71.9 jit_solution(8782982920478460857)
XLA Ops:
  0.0 71.1 %shard_map.46 = bf16[32,16,256]{2,1,0:T(8,128)(2,1)S(1)} custom-call(s32[24]{0:T(128)} %owners_hbm.1, s32[2,12]{1,0:T(2,128)} %bitcast.7, bf16[1,12,96,512]{3,2,1,0:T(8,128)(2,1)} %acts_hbm.1, bf16[1,12,96,512]{3,2,1,0:T(8,128)(2,1)} %cots_hbm.1), custom_call_target="tpu_custom_call" | custom-call | tf_op jit(solution)/shard_map/pallas_call | solution.py:404
  71.1 0.9 %bitcast_convert_fusion = f32[32,2,8,256]{3,2,1,0:T(8,128)} fusion(bf16[32,16,256]{2,1,0:T(8,128)(2,1)S(1)} %shard_map.46), kind=kLoop, calls=%fused_computation | loop fusion | flops 131072 | bytes 786432 | tf_op jit(solution)/shard_map/reshape | solution.py:451

commit v3 on v2

--- a/solution.py
+++ b/solution.py
@@ -10,9 +10,10 @@
 
 MESH = pl.DeviceIdType.MESH
 DAMPING = 0.01
+ROOT = [value / 4096.0 for value in (6400, -4405, 3125, -1250, 250, -25, 1)]
 CHUNKS = 8
 LOADS = 4
-STRIPS = 4
+STRIPS = 2
 
 ROWS_BY_ROWS = (((1,), (1,)), ((), ()))
 COLUMNS_BY_COLUMNS = (((0,), (0,)), ((), ()))
@@ -26,10 +27,10 @@
     n_z, n_x, n_y,
     owners_hbm, shapes_hbm, acts_hbm, cots_hbm, out_ref,
     owners_ref, shapes_ref, acts_ref, cots_ref, staged, paired, part, ring, swapped, grad,
-    stat, coupled, coupled_bf, work, work_bf, left, right,
+    stat, stat_bf, second, second_bf, third_bf, rest_bf, left, right,
     weighted, weighted_out, rows_own, rows_shift, rows_out,
     loaded, pair_send, pair_recv, ring_send, ring_recv,
-    swap_send, swap_recv, root_send, root_recv, shift_send, shift_recv, rows_send, rows_recv,
+    swap_send, swap_recv, root_send, root_recv, shift_send, shift_recv, rows_send, rows_recv, token,
 ):
     tokens, width = acts_ref.shape[1:]
     half = width // 2
@@ -63,13 +64,25 @@
         load.start()
 
     barrier = pltpu.get_barrier_semaphore()
-    for neighbour in (partner, above, below):
+    neighbours = [partner, above, below, (peer(0, 1), rep), (peer(0, n_y - 1), rep)]
+    if n_x > 1:
+        neighbours += [(peer(1, 0), rep), (peer(n_x - 1, 0), rep)]
+    for neighbour in neighbours:
         pl.semaphore_signal(barrier, inc=1, device_id=neighbour, device_id_type=MESH)
 
-    @pl.loop(1, n_shard)
-    def _(step):
-        to = (peer(step // n_y, lax.rem(step, n_y)), rep)
-        pl.semaphore_signal(barrier, inc=1, device_id=to, device_id_type=MESH)
+    rounds_y = n_y // 2 - 1
+    rounds = rounds_y + n_x // 2
+
+    def greet(turn):
+        turn = jnp.int32(turn)
+        along = jnp.minimum(jnp.maximum(rounds_y - turn, 0), 1)
+        across = 1 - along
+        for side, to in enumerate((peer(across, along), peer(n_x - across, n_y - along))):
+            pl.semaphore_signal(token.at[turn, side], inc=1, device_id=(to, rep), device_id_type=MESH)
+
+    def hear(turn):
+        for side in range(2):
+            pl.semaphore_wait(token.at[turn, side], 1)
 
     for load in loads:
         load.wait()
@@ -87,26 +100,23 @@
 
     own_tokens = pl.ds(pl.multiple_of(core * tokens, tokens), tokens)
 
+    def pair_copy(item):
+        return pltpu.make_async_remote_copy(
+            src_ref=staged.at[item],
+            dst_ref=paired.at[item, own_tokens, :],
+            send_sem=pair_send.at[item],
+            recv_sem=pair_recv.at[item],
+            device_id=partner,
+            device_id_type=MESH,
+        )
+
+    pl.semaphore_wait(barrier, len(neighbours))
+
     @pl.loop(0, n_hops + 1)
     def _(item):
         block = block_at(z - sign * (n_hops - item))
         staged[item, :, :width] = cots_ref[block]
         staged[item, :, width:] = acts_ref[block]
-
-    def pair_copy(item):
-        return pltpu.make_async_remote_copy(
-            src_ref=staged.at[item],
-            dst_ref=paired.at[item, own_tokens, :],
-            send_sem=pair_send.at[item],
-            recv_sem=pair_recv.at[item],
-            device_id=partner,
-            device_id_type=MESH,
-        )
-
-    pl.semaphore_wait(barrier, 3 + n_shard - 1)
-
-    @pl.loop(0, n_hops + 1)
-    def _(item):
         pair_copy(item).start()
 
     def partial(item):
@@ -138,6 +148,8 @@
     for chunk in range(few):
         ring[0, span_of(core * few + chunk), :] = part[chunk * rows : (chunk + 1) * rows, :].astype(jnp.bfloat16)
         ring_copy(0, core * few + chunk).start()
+
+    greet(0)
 
     def all_rows(item):
         outputs = partial(item)
@@ -158,11 +170,20 @@
     for chunk in range(few):
         forward(1, core * few + chunk)
 
+    hear(0)
+    if rounds > 1:
+        greet(1)
+
     @pl.loop(2, n_hops)
     def _(step):
         all_rows(step)
         for chunk in range(CHUNKS):
             forward(step, chunk)
+        hear(step - 1)
+
+        @pl.when(step < rounds)
+        def _():
+            greet(step)
 
     all_rows(n_hops)
 
@@ -200,15 +221,19 @@
     deep = width // STRIPS
     strips = [slice(i * deep, (i + 1) * deep) for i in range(STRIPS)]
 
+    def keep(strip, values):
+        stat[strip, :] = values
+        stat_bf[strip, :] = values.astype(jnp.bfloat16)
+
     @pl.when(core == 0)
     def _():
         for strip in strips:
-            stat[strip, :] = dot(grad[strip, :], grad[...], ROWS_BY_ROWS)
+            keep(strip, dot(grad[strip, :], grad[...], ROWS_BY_ROWS))
 
     @pl.when(core == 1)
     def _():
         for strip in strips:
-            stat[strip, :] = dot(grad[:, strip], grad[...], COLUMNS_BY_COLUMNS)
+            keep(strip, dot(grad[:, strip], grad[...], COLUMNS_BY_COLUMNS))
 
     def diagonal(strip):
         return (
@@ -216,6 +241,8 @@
             == lax.broadcasted_iota(jnp.int32, (deep, width), 1)
         )
 
+    for strip in strips:
+        second[strip, :] = dot(stat_bf[strip, :], stat_bf[...])
     squares = jnp.zeros((1, 1), jnp.float32)
     trace = jnp.zeros((1, 1), jnp.float32)
     for strip in strips:
@@ -228,26 +255,24 @@
     scale = lax.rsqrt(jnp.sqrt(jnp.sqrt(norm_squared)))
 
     for strip in strips:
-        values = (stat[strip, :] + jnp.where(diagonal(strip), damping, 0.0)) * inverse
-        coupled[strip, :] = values
-        coupled_bf[strip, :] = values.astype(jnp.bfloat16)
+        eye = jnp.where(diagonal(strip), damping, 0.0)
+        values = stat[strip, :]
+        square = (second[strip, :] + damping * (2.0 * values + eye)) * inverse * inverse
+        values = (values + eye) * inverse
+        stat[strip, :] = values
+        stat_bf[strip, :] = values.astype(jnp.bfloat16)
+        second[strip, :] = square
+        second_bf[strip, :] = square.astype(jnp.bfloat16)
     for strip in strips:
-        square = dot(coupled_bf[strip, :], coupled_bf[...])
-        values = 0.0625 * square - 0.625 * coupled[strip, :]
-        stat[strip, :] = values
-        work_bf[0, strip, :] = values.astype(jnp.bfloat16)
-    for strip in strips:
-        square = dot(work_bf[0, strip, :], work_bf[0])
-        work_bf[1, strip, :] = (square + 3.125 * stat[strip, :]).astype(jnp.bfloat16)
-    for strip in strips:
-        values = dot(work_bf[1, strip, :], coupled_bf[...]) + 2.44140625 * coupled[strip, :]
-        work[strip, :] = values
-        work_bf[0, strip, :] = values.astype(jnp.bfloat16)
+        cube = dot(second_bf[strip, :], stat_bf[...])
+        third_bf[strip, :] = cube.astype(jnp.bfloat16)
+        one, two = stat[strip, :], second[strip, :]
+        rest_bf[strip, :] = (ROOT[4] * one + ROOT[5] * two + ROOT[6] * cube).astype(jnp.bfloat16)
+        lead = ROOT[1] * one + ROOT[2] * two + ROOT[3] * cube
+        second[strip, :] = lead + jnp.where(diagonal(strip), ROOT[0], 0.0)
 
     def root(strip):
-        values = 0.0625 * dot(coupled_bf[strip, :], work_bf[0])
-        values = values - 0.3125 * (coupled[strip, :] + work[strip, :])
-        values = values + jnp.where(diagonal(strip), 1.5625, 0.0)
+        values = second[strip, :] + dot(third_bf[strip, :], rest_bf[...])
         return (values * scale).astype(jnp.bfloat16)
 
     def right_copy(index):
@@ -289,14 +314,13 @@
             right_copy(index).wait_recv()
 
     piece = half // n_shard
-    spread = half // n_x
 
     def update_rows(into):
+        values = dot(weighted[...], right[...]) * math.sqrt(width)
+        values = values.reshape(n_x, n_y, piece, width)
         for across in range(n_x):
-            values = dot(weighted[across * spread : (across + 1) * spread, :], right[...]) * math.sqrt(width)
-            values = values.reshape(n_y, piece, width)
-            values = jnp.concatenate([values[:, :, :half], values[:, :, half:]], axis=1)
-            into[:, across] = values.astype(jnp.bfloat16)
+            folded = jnp.concatenate([values[across, :, :, :half], values[across, :, :, half:]], axis=1)
+            into[:, across] = folded.astype(jnp.bfloat16)
 
     far_first = sorted(range(n_y), key=lambda along: -min(along, n_y - along))
     far_first_x = sorted(range(n_x), key=lambda across: -min(across, n_x - across))
@@ -418,10 +442,11 @@
             pltpu.VMEM((width, width), bf16),
             pltpu.VMEM((width, width), bf16),
             pltpu.VMEM((width, width), f32),
+            pltpu.VMEM((width, width), bf16),
             pltpu.VMEM((width, width), f32),
             pltpu.VMEM((width, width), bf16),
-            pltpu.VMEM((width, width), f32),
-            pltpu.VMEM((2, width, width), bf16),
+            pltpu.VMEM((width, width), bf16),
+            pltpu.VMEM((width, width), bf16),
             pltpu.VMEM((2, half, width), bf16),
             pltpu.VMEM((width, width), bf16),
             pltpu.VMEM((half, width), bf16),
@@ -442,6 +467,7 @@
             dma((n_y,)),
             dma((n_x, n_y)),
             dma((n_x, n_y)),
+            pltpu.SemaphoreType.REGULAR((n_z // 2 - 1, 2)),
         ],
         compiler_params=pltpu.CompilerParams(
             collective_id=0, has_side_effects=True, vmem_limit_bytes=62 * 1024 * 1024

time: 72.1 us -> 69.8 us (0.968)
  the two profiles are of different devices: /device:TPU:8 before, /device:TPU:16 now
where the time goes in v3:
time: 69.8 us; the launch traced here: 69.7 us
  Pallas kernels  68.8 us (99%)
  other arithmetic  0.85 us (1%)
    pallas_call x1, Pallas kernels, local(): pl.pallas_call(functools.partial(kernel, n_z, n_x, n_y), out_shape=pltpu....  68.8 us

profile of v3, /device:TPU:16, one launch (start us, length us, event | category | flops | bytes accessed | tf_op | source)
XLA Modules:
  0.0 69.7 jit_solution(3768040994922035979)
XLA Ops:
  0.0 68.8 %shard_map.46 = bf16[32,16,256]{2,1,0:T(8,128)(2,1)S(1)} custom-call(s32[24]{0:T(128)} %owners_hbm.1, s32[2,12]{1,0:T(2,128)} %bitcast.7, bf16[1,12,96,512]{3,2,1,0:T(8,128)(2,1)} %acts_hbm.1, bf16[1,12,96,512]{3,2,1,0:T(8,128)(2,1)} %cots_hbm.1), custom_call_target="tpu_custom_call" | custom-call | tf_op jit(solution)/shard_map/pallas_call | solution.py:428
  68.8 0.9 %bitcast_convert_fusion = f32[32,2,8,256]{3,2,1,0:T(8,128)} fusion(bf16[32,16,256]{2,1,0:T(8,128)(2,1)S(1)} %shard_map.46), kind=kLoop, calls=%fused_computation | loop fusion | flops 131072 | bytes 786432 | tf_op jit(solution)/shard_map/reshape | solution.py:477

commit v4 on v3

--- a/solution.py
+++ b/solution.py
@@ -11,8 +11,8 @@
 MESH = pl.DeviceIdType.MESH
 DAMPING = 0.01
 ROOT = [value / 4096.0 for value in (6400, -4405, 3125, -1250, 250, -25, 1)]
-CHUNKS = 8
-LOADS = 4
+CHUNKS = 4
+LOADS = 1
 STRIPS = 2
 
 ROWS_BY_ROWS = (((1,), (1,)), ((), ()))
@@ -29,8 +29,7 @@
     owners_ref, shapes_ref, acts_ref, cots_ref, staged, paired, part, ring, swapped, grad,
     stat, stat_bf, second, second_bf, third_bf, rest_bf, left, right,
     weighted, weighted_out, rows_own, rows_shift, rows_out,
-    loaded, pair_send, pair_recv, ring_send, ring_recv,
-    swap_send, swap_recv, root_send, root_recv, shift_send, shift_recv, rows_send, rows_recv, token,
+    pool, pair_recv, ring_recv, swap_recv, root_send, root_recv, shift_send, shift_recv, rows_recv, token,
 ):
     tokens, width = acts_ref.shape[1:]
     half = width // 2
@@ -53,13 +52,13 @@
 
     span = n_z // LOADS
     loads = [
-        pltpu.make_async_copy(owners_hbm, owners_ref, loaded.at[2 * LOADS]),
-        pltpu.make_async_copy(shapes_hbm, shapes_ref, loaded.at[2 * LOADS + 1]),
+        pltpu.make_async_copy(owners_hbm, owners_ref, pool.at[2 * LOADS]),
+        pltpu.make_async_copy(shapes_hbm, shapes_ref, pool.at[2 * LOADS + 1]),
     ]
     for index in range(LOADS):
         blocks = pl.ds(index * span, span)
-        loads.append(pltpu.make_async_copy(cots_hbm.at[0, blocks], cots_ref.at[blocks], loaded.at[index]))
-        loads.append(pltpu.make_async_copy(acts_hbm.at[0, blocks], acts_ref.at[blocks], loaded.at[LOADS + index]))
+        loads.append(pltpu.make_async_copy(cots_hbm.at[0, blocks], cots_ref.at[blocks], pool.at[index]))
+        loads.append(pltpu.make_async_copy(acts_hbm.at[0, blocks], acts_ref.at[blocks], pool.at[LOADS + index]))
     for load in loads:
         load.start()
 
@@ -104,7 +103,7 @@
         return pltpu.make_async_remote_copy(
             src_ref=staged.at[item],
             dst_ref=paired.at[item, own_tokens, :],
-            send_sem=pair_send.at[item],
+            send_sem=shift_send.at[item],
             recv_sem=pair_recv.at[item],
             device_id=partner,
             device_id_type=MESH,
@@ -136,7 +135,7 @@
         return pltpu.make_async_remote_copy(
             src_ref=ring.at[step, span_of(chunk), :],
             dst_ref=ring.at[step + 1, span_of(chunk), :],
-            send_sem=ring_send.at[step, chunk],
+            send_sem=pool.at[step * CHUNKS + chunk],
             recv_sem=ring_recv.at[step, chunk],
             device_id=ring_to,
             device_id_type=MESH,
@@ -195,7 +194,7 @@
         return pltpu.make_async_remote_copy(
             src_ref=ring.at[n_hops, span_of(chunk), :],
             dst_ref=swapped.at[span_of(chunk), :],
-            send_sem=swap_send.at[chunk],
+            send_sem=pool.at[n_hops * CHUNKS + chunk],
             recv_sem=swap_recv.at[chunk],
             device_id=partner,
             device_id_type=MESH,
@@ -313,6 +312,21 @@
         for index in range(STRIPS):
             right_copy(index).wait_recv()
 
+    @pl.loop(0, n_hops + 1)
+    def _(item):
+        pair_copy(item).wait_send()
+
+    for chunk in range(few):
+        ring_copy(0, core * few + chunk).wait_send()
+
+    @pl.loop(1, n_hops)
+    def _(step):
+        for chunk in range(CHUNKS):
+            ring_copy(step, chunk).wait_send()
+
+    for chunk in range(CHUNKS):
+        swap_copy(chunk).wait_send()
+
     piece = half // n_shard
 
     def update_rows(into):
@@ -342,13 +356,13 @@
         return pltpu.make_async_remote_copy(
             src_ref=rows_out.at[column(along), lax.rem(x + across, n_x)],
             dst_ref=out_ref.at[shard],
-            send_sem=rows_send.at[across, along],
+            send_sem=pool.at[across * n_y + along],
             recv_sem=rows_recv.at[across, along],
             device_id=(peer(across, along), rep),
             device_id_type=MESH,
         )
 
-    own_copy = pltpu.make_async_copy(rows_out.at[y, x], out_ref.at[shard], rows_send.at[0, 0])
+    own_copy = pltpu.make_async_copy(rows_out.at[y, x], out_ref.at[shard], pool.at[0])
 
     def send_rows(along):
         for across in far_first_x:
@@ -381,21 +395,6 @@
     @pl.loop(1, n_shard)
     def _(step):
         rows_copy(step // n_y, lax.rem(step, n_y)).wait_recv()
-
-    @pl.loop(0, n_hops + 1)
-    def _(item):
-        pair_copy(item).wait_send()
-
-    for chunk in range(few):
-        ring_copy(0, core * few + chunk).wait_send()
-
-    @pl.loop(1, n_hops)
-    def _(step):
-        for chunk in range(CHUNKS):
-            ring_copy(step, chunk).wait_send()
-
-    for chunk in range(CHUNKS):
-        swap_copy(chunk).wait_send()
 
     @pl.when(core == 1)
     def _():
@@ -454,18 +453,14 @@
             pieces,
             pieces,
             pieces,
-            dma((2 * LOADS + 2,)),
-            dma((n_hops + 1,)),
+            dma((max(n_shard, (n_hops + 1) * CHUNKS),)),
             dma((n_hops + 1,)),
             dma((n_hops, CHUNKS)),
-            dma((n_hops, CHUNKS)),
-            dma((CHUNKS,)),
             dma((CHUNKS,)),
             dma((STRIPS + 1,)),
             dma((STRIPS + 1,)),
+            dma((max(n_y, n_hops + 1),)),
             dma((n_y,)),
-            dma((n_y,)),
-            dma((n_x, n_y)),
             dma((n_x, n_y)),
             pltpu.SemaphoreType.REGULAR((n_z // 2 - 1, 2)),
         ],

time: 69.8 us -> 69.4 us (level)
  no operation moved by 1% of the time
where the time goes in v4:
time: 69.4 us; the launch traced here: 69.2 us
  Pallas kernels  68.4 us (99%)
  other arithmetic  0.85 us (1%)
    pallas_call x1, Pallas kernels, local(): pl.pallas_call(functools.partial(kernel, n_z, n_x, n_y), out_shape=pltpu....  68.4 us

profile of v4, /device:TPU:16, one launch (start us, length us, event | category | flops | bytes accessed | tf_op | source)
XLA Modules:
  0.0 69.2 jit_solution(8530502074759958092)
XLA Ops:
  0.0 68.4 %shard_map.46 = bf16[32,16,256]{2,1,0:T(8,128)(2,1)S(1)} custom-call(s32[24]{0:T(128)} %owners_hbm.1, s32[2,12]{1,0:T(2,128)} %bitcast.7, bf16[1,12,96,512]{3,2,1,0:T(8,128)(2,1)} %acts_hbm.1, bf16[1,12,96,512]{3,2,1,0:T(8,128)(2,1)} %cots_hbm.1), custom_call_target="tpu_custom_call" | custom-call | tf_op jit(solution)/shard_map/pallas_call | solution.py:427
  68.4 0.9 %bitcast_convert_fusion = f32[32,2,8,256]{3,2,1,0:T(8,128)} fusion(bf16[32,16,256]{2,1,0:T(8,128)(2,1)S(1)} %shard_map.46), kind=kLoop, calls=%fused_computation | loop fusion | flops 131072 | bytes 786432 | tf_op jit(solution)/shard_map/reshape | solution.py:472

commit v5 on v4

--- a/solution.py
+++ b/solution.py
@@ -357,7 +357,7 @@
             src_ref=rows_out.at[column(along), lax.rem(x + across, n_x)],
             dst_ref=out_ref.at[shard],
             send_sem=pool.at[across * n_y + along],
-            recv_sem=rows_recv.at[across, along],
+            recv_sem=rows_recv.at[along],
             device_id=(peer(across, along), rep),
             device_id_type=MESH,
         )
@@ -392,9 +392,17 @@
 
     own_copy.wait()
 
-    @pl.loop(1, n_shard)
-    def _(step):
-        rows_copy(step // n_y, lax.rem(step, n_y)).wait_recv()
+    for along in range(n_y):
+        count = n_x - (along == 0)
+        if count:
+            pltpu.make_async_remote_copy(
+                src_ref=rows_out.at[0, pl.ds(0, count)],
+                dst_ref=out_ref.at[pl.ds(0, count)],
+                send_sem=pool.at[0],
+                recv_sem=rows_recv.at[along],
+                device_id=partner,
+                device_id_type=MESH,
+            ).wait_recv()
 
     @pl.when(core == 1)
     def _():
@@ -461,7 +469,7 @@
             dma((STRIPS + 1,)),
             dma((max(n_y, n_hops + 1),)),
             dma((n_y,)),
-            dma((n_x, n_y)),
+            dma((n_y,)),
             pltpu.SemaphoreType.REGULAR((n_z // 2 - 1, 2)),
         ],
         compiler_params=pltpu.CompilerParams(

time: 69.4 us -> 69.2 us (level)
  no operation moved by 1% of the time
where the time goes in v5:
time: 69.2 us; the launch traced here: 69 us
  Pallas kernels  68.1 us (98%)
  other arithmetic  0.85 us (1%)
    pallas_call x1, Pallas kernels, local(): pl.pallas_call(functools.partial(kernel, n_z, n_x, n_y), out_shape=pltpu....  68.1 us

profile of v5, /device:TPU:16, one launch (start us, length us, event | category | flops | bytes accessed | tf_op | source)
XLA Modules:
  0.0 69.0 jit_solution(12748123511537062389)
XLA Ops:
  0.0 68.1 %shard_map.46 = bf16[32,16,256]{2,1,0:T(8,128)(2,1)S(1)} custom-call(s32[24]{0:T(128)} %owners_hbm.1, s32[2,12]{1,0:T(2,128)} %bitcast.7, bf16[1,12,96,512]{3,2,1,0:T(8,128)(2,1)} %acts_hbm.1, bf16[1,12,96,512]{3,2,1,0:T(8,128)(2,1)} %cots_hbm.1), custom_call_target="tpu_custom_call" | custom-call | tf_op jit(solution)/shard_map/pallas_call | solution.py:435
  68.1 0.9 %bitcast_convert_fusion = f32[32,2,8,256]{3,2,1,0:T(8,128)} fusion(bf16[32,16,256]{2,1,0:T(8,128)(2,1)S(1)} %shard_map.46), kind=kLoop, calls=%fused_computation | loop fusion | flops 131072 | bytes 786432 | tf_op jit(solution)/shard_map/reshape | solution.py:480
